TPU v7x, 256 devices: a whole 4x4x8 slice. The times are simulated.
256 devices in a mesh: seq: 8 (over x, core), ctx: 32 (over y, z).
Axes of the slice: x: 4, y: 4, z: 8, core: 2. Of those that a mesh axis runs over, the one named last changes fastest.
Arguments:
- queries: bfloat16 [65536, 2048], P(('seq', 'ctx')), parts along dimension 0, may hold values from -216 to 216
- keys: bfloat16 [65536, 512], P(('seq', 'ctx')), parts along dimension 0, may hold values from -6 to 6
- values: bfloat16 [65536, 512], P(('seq', 'ctx')), parts along dimension 0, may hold values from -6 to 6
- out_grad: bfloat16 [65536, 2048], P(('seq', 'ctx')), parts along dimension 0, may hold values from -6 to 6
- block_docs: int32 [512], P('seq'), parts along dimension 0, may hold values from 0 to 31, never falling along the last dimension, each value on 1 to 4 neighbouring positions
Outputs:
- attended: bfloat16 [65536, 2048], P(('seq', 'ctx')), parts along dimension 0
- query_grad: bfloat16 [65536, 2048], P(('seq', 'ctx')), parts along dimension 0
- key_grad: bfloat16 [65536, 512], P(('seq', 'ctx')), parts along dimension 0
- value_grad: bfloat16 [65536, 512], P(('seq', 'ctx')), parts along dimension 0
There are 8 independent parts, one for each index of `seq`. A program takes and returns all parts, laid end to end along the dimension named above; each array names one. Nothing has to cross between parts.
Inputs may be any that keep to these rules, and one draw needn't show every extreme that they name: `block_docs`: documents are runs of 1 to 4 consecutive blocks, numbered from 0 and never falling; some document has exactly 4 blocks.
All inputs are finite; a program needn't handle non-finite values.
Results may differ from a plain program's by a relative error of at most 0.015.
Values may be sent and summed in bfloat16 or wider, within the bound.
A program may use at most 128 MiB of HBM per device.

v0:
```python
import math

import jax
import jax.numpy as jnp
from jax import lax
from jax.experimental import pallas as pl
from jax.experimental.pallas import tpu as pltpu
from jax.sharding import PartitionSpec as P

HEAD_DIM = 128
HEADS = 16
KV_HEADS = 4
GROUP = HEADS // KV_HEADS
BLOCK = 128
MOST = 4
ROWS = 256
LEAD = (MOST - 1) * BLOCK
WINDOW = MOST * BLOCK
SCALE = 1.0 / math.sqrt(HEAD_DIM)
SCALE_LOG2 = math.log2(math.e) / math.sqrt(HEAD_DIM)
FAR = 1e30
MESH = pl.DeviceIdType.MESH

NT = (((1,), (1,)), ((), ()))
TN = (((0,), (0,)), ((), ()))
NN = (((1,), (0,)), ((), ()))


def dot(lhs, rhs, dims):
    return lax.dot_general(lhs, rhs, dims, preferred_element_type=jnp.float32)


def block_rows(value, index):
    return value[index * BLOCK : (index + 1) * BLOCK]


def attend(keys, values, queries, grads, live):
    scores = dot(keys, queries, NT)
    weight_grad = dot(values, grads, NT)
    width = queries.shape[0]
    key_ids = lax.broadcasted_iota(jnp.int32, (BLOCK, width), 0)
    query_ids = lax.broadcasted_iota(jnp.int32, (BLOCK, width), 1) % BLOCK
    tiles = [block_rows(scores, t) for t in range(MOST)]
    tiles[-1] = jnp.where(key_ids <= query_ids, tiles[-1], -FAR)
    top = jnp.max(tiles[-1], axis=0, keepdims=True)
    for t in range(MOST - 1):
        top = jnp.maximum(top, jnp.where(live[t], jnp.max(tiles[t], axis=0, keepdims=True), -FAR))
    top = top * SCALE_LOG2
    shifts = [jnp.where(live[t], top, FAR) for t in range(MOST - 1)] + [top]
    exps = [jnp.exp2(tiles[t] * SCALE_LOG2 - shifts[t]) for t in range(MOST)]
    total = sum(jnp.sum(part, axis=0, keepdims=True) for part in exps)
    weights = jnp.concatenate(exps, 0) * (1.0 / total)
    weights_b = weights.astype(jnp.bfloat16)
    row_dot = jnp.sum(weights * weight_grad, axis=0, keepdims=True)
    score_grad = (weights * (weight_grad - row_dot)).astype(jnp.bfloat16)
    attended = jnp.transpose(dot(values, weights_b, TN).astype(jnp.bfloat16))
    query_grad = jnp.transpose((dot(keys, score_grad, TN) * SCALE).astype(jnp.bfloat16))
    key_part = dot(score_grad, queries, NN) * SCALE
    value_part = dot(weights_b, grads, NN)
    return attended, query_grad, key_part, value_part


def kernel(
    docs, q_hbm, k_hbm, v_hbm, g_hbm, att_hbm, dq_hbm, dk_hbm, dv_hbm,
    q_buf, g_buf, kv_buf, att_buf, dq_buf, out_buf, part, own_part, send_buf, got_buf,
    load_sem, kv_sem, store_sem, out_sem,
    own_send, own_recv, fwd_send, fwd_recv, ret_send, ret_recv,
):
    seq = lax.axis_index("seq")
    me = lax.axis_index("ctx")
    last = lax.axis_size("ctx") - 1
    has_prev, has_next = me > 0, me < last
    prev, following = jnp.maximum(me - 1, 0), jnp.minimum(me + 1, last)

    barrier = pltpu.get_barrier_semaphore()

    @pl.when(has_prev)
    def _():
        pl.semaphore_signal(barrier, inc=1, device_id=(seq, prev), device_id_type=MESH)

    kv_loads = []
    for h in range(KV_HEADS):
        for n, ref in enumerate((k_hbm, v_hbm)):
            copy = pltpu.make_async_copy(
                ref.at[:, pl.ds(h * HEAD_DIM, HEAD_DIM)],
                kv_buf.at[h, n, pl.ds(LEAD, ROWS)],
                kv_sem.at[h, n],
            )
            copy.start()
            kv_loads.append(copy)
    loads = [
        pltpu.make_async_copy(q_hbm, q_buf, load_sem.at[0]),
        pltpu.make_async_copy(g_hbm, g_buf, load_sem.at[1]),
    ]
    for copy in loads:
        copy.start()

    def own(h, b):
        return pltpu.make_async_remote_copy(
            kv_buf.at[h, :, pl.ds(LEAD + b * BLOCK, BLOCK)],
            kv_buf.at[h, :, pl.ds((1 + b) * BLOCK, BLOCK)],
            own_send.at[h, b], own_recv.at[h, b],
            device_id=(seq, following), device_id_type=MESH,
        )

    def forward(h):
        return pltpu.make_async_remote_copy(
            kv_buf.at[h, :, pl.ds(2 * BLOCK, BLOCK)],
            kv_buf.at[h, :, pl.ds(0, BLOCK)],
            fwd_send.at[h], fwd_recv.at[h],
            device_id=(seq, following), device_id_type=MESH,
        )

    def give_back(h, b):
        return pltpu.make_async_remote_copy(
            send_buf.at[h, b], got_buf.at[h, b],
            ret_send.at[h, b], ret_recv.at[h, b],
            device_id=(seq, prev), device_id_type=MESH,
        )

    @pl.when(has_next)
    def _():
        pl.semaphore_wait(barrier, 1)

    for copy in kv_loads:
        copy.wait()

    @pl.when(has_next)
    def _():
        for h in range(2):
            own(h, 1).start()
            own(h, 0).start()

    @pl.when(jnp.logical_not(has_prev))
    def _():
        kv_buf[:, :, :LEAD] = jnp.zeros((KV_HEADS, 2, LEAD, HEAD_DIM), jnp.bfloat16)

    for copy in loads:
        copy.wait()

    def live(slot):
        own_doc = docs[2 * me + slot]
        result = []
        for t in range(MOST - 1):
            place = 2 * me + slot + t - (MOST - 1)
            result.append((place >= 0) & (docs[jnp.maximum(place, 0)] == own_doc))
        return result

    lives = [live(0), live(1)]

    def compute(h, slot):
        rows = slice(slot * BLOCK, (slot + 1) * BLOCK)
        lanes = [slice((h * GROUP + j) * HEAD_DIM, (h * GROUP + j + 1) * HEAD_DIM) for j in range(GROUP)]
        queries = jnp.concatenate([q_buf[rows, lane] for lane in lanes], 0)
        grads = jnp.concatenate([g_buf[rows, lane] for lane in lanes], 0)
        keys = kv_buf[h, 0, slot * BLOCK : slot * BLOCK + WINDOW]
        values = kv_buf[h, 1, slot * BLOCK : slot * BLOCK + WINDOW]
        attended, query_grad, key_part, value_part = attend(keys, values, queries, grads, lives[slot])
        for j, lane in enumerate(lanes):
            att_buf[rows, lane] = block_rows(attended, j)
            dq_buf[rows, lane] = block_rows(query_grad, j)
        return key_part, value_part

    def relay(h):
        @pl.when(has_next)
        def _():
            give_back(h, 0).wait_recv()
            part[h % 2] += got_buf[h, 0].astype(jnp.float32)

        @pl.when(has_prev)
        def _():
            send_buf[h, 2] = part[h % 2].astype(jnp.bfloat16)
            give_back(h, 2).start()

    def stores(h):
        lanes = pl.ds(h * HEAD_DIM, HEAD_DIM)
        return [
            pltpu.make_async_copy(out_buf.at[h, n], ref.at[:, lanes], out_sem.at[h, n])
            for n, ref in enumerate((dk_hbm, dv_hbm))
        ]

    def finish(h):
        @pl.when(has_next)
        def _():
            for b in range(2):
                give_back(h, 1 + b).wait_recv()
                own_part[h % 2, b] += got_buf[h, 1 + b].astype(jnp.float32)

        for n in range(2):
            for b in range(2):
                out_buf[h, n, b * BLOCK : (b + 1) * BLOCK] = own_part[h % 2, b, n].astype(jnp.bfloat16)
        for copy in stores(h):
            copy.start()

    wide = GROUP * HEAD_DIM

    def wide_stores(h):
        lanes = pl.ds(h * wide, wide)
        return [
            pltpu.make_async_copy(att_buf.at[:, lanes], att_hbm.at[:, lanes], store_sem.at[h, 0]),
            pltpu.make_async_copy(dq_buf.at[:, lanes], dq_hbm.at[:, lanes], store_sem.at[h, 1]),
        ]

    for h in range(KV_HEADS):

        @pl.when(has_prev)
        def _(h=h):
            own(h, 1).wait_recv()

        @pl.when(has_next)
        def _(h=h):
            forward(h).start()
            if h + 2 < KV_HEADS:
                own(h + 2, 1).start()
                own(h + 2, 0).start()

        @pl.when(has_prev)
        def _(h=h):
            own(h, 0).wait_recv()

        later = compute(h, 1)
        for n in range(2):
            part[h % 2, n] = block_rows(later[n], 1)
            own_part[h % 2, 0, n] = block_rows(later[n], 2)
            own_part[h % 2, 1, n] = block_rows(later[n], 3)
            send_f32 = block_rows(later[n], 0)
            own_part[h % 2, 2, n] = send_f32

        if h > 0:
            relay(h - 1)

        @pl.when(has_prev)
        def _(h=h):
            forward(h).wait_recv()

        earlier = compute(h, 0)
        for n in range(2):
            part[h % 2, n] += block_rows(earlier[n], 2)
            own_part[h % 2, 0, n] += block_rows(earlier[n], 3)
            send_buf[h, 0, n] = block_rows(earlier[n], 0).astype(jnp.bfloat16)
            send_buf[h, 1, n] = (block_rows(earlier[n], 1) + own_part[h % 2, 2, n]).astype(jnp.bfloat16)

        @pl.when(has_prev)
        def _(h=h):
            give_back(h, 0).start()
            give_back(h, 1).start()

        for copy in wide_stores(h):
            copy.start()
        if h > 0:
            finish(h - 1)

    relay(KV_HEADS - 1)
    finish(KV_HEADS - 1)

    @pl.when(has_next)
    def _():
        for h in range(KV_HEADS):
            own(h, 1).wait_send()
            own(h, 0).wait_send()
            forward(h).wait_send()

    @pl.when(has_prev)
    def _():
        for h in range(KV_HEADS):
            for b in range(3):
                give_back(h, b).wait_send()

    for h in range(KV_HEADS):
        for copy in wide_stores(h) + stores(h):
            copy.wait()


def on_device(queries, keys, values, out_grad, block_docs):
    hbm = pl.BlockSpec(memory_space=pl.ANY)
    dma = pltpu.SemaphoreType.DMA
    bf16, f32 = jnp.bfloat16, jnp.float32
    return pl.pallas_call(
        kernel,
        out_shape=[
            jax.ShapeDtypeStruct(queries.shape, bf16),
            jax.ShapeDtypeStruct(queries.shape, bf16),
            jax.ShapeDtypeStruct(keys.shape, bf16),
            jax.ShapeDtypeStruct(keys.shape, bf16),
        ],
        in_specs=[pl.BlockSpec(memory_space=pltpu.SMEM)] + [hbm] * 4,
        out_specs=[hbm] * 4,
        scratch_shapes=[
            pltpu.VMEM((ROWS, HEADS * HEAD_DIM), bf16),
            pltpu.VMEM((ROWS, HEADS * HEAD_DIM), bf16),
            pltpu.VMEM((KV_HEADS, 2, LEAD + ROWS, HEAD_DIM), bf16),
            pltpu.VMEM((ROWS, HEADS * HEAD_DIM), bf16),
            pltpu.VMEM((ROWS, HEADS * HEAD_DIM), bf16),
            pltpu.VMEM((KV_HEADS, 2, ROWS, HEAD_DIM), bf16),
            pltpu.VMEM((2, 2, BLOCK, HEAD_DIM), f32),
            pltpu.VMEM((2, 3, 2, BLOCK, HEAD_DIM), f32),
            pltpu.VMEM((KV_HEADS, 3, 2, BLOCK, HEAD_DIM), bf16),
            pltpu.VMEM((KV_HEADS, 3, 2, BLOCK, HEAD_DIM), bf16),
            dma((2,)),
            dma((KV_HEADS, 2)),
            dma((KV_HEADS, 2)),
            dma((KV_HEADS, 2)),
            dma((KV_HEADS, 2)),
            dma((KV_HEADS, 2)),
            dma((KV_HEADS,)),
            dma((KV_HEADS,)),
            dma((KV_HEADS, 3)),
            dma((KV_HEADS, 3)),
        ],
        compiler_params=pltpu.CompilerParams(
            collective_id=0, has_side_effects=True, vmem_limit_bytes=62 * 1024 * 1024
        ),
        cost_estimate=pl.CostEstimate(
            flops=3_300_000_000, bytes_accessed=5_500_000, transcendentals=2_100_000
        ),
    )(block_docs, queries, keys, values, out_grad)


def solution(mesh):
    tokens = P(("seq", "ctx"), None)
    return jax.shard_map(
        on_device,
        mesh=mesh,
        in_specs=(tokens, tokens, tokens, tokens, P("seq")),
        out_specs=(tokens, tokens, tokens, tokens),
        check_vma=False,
    )
```

profile of v0, /device:TPU:12, one launch (start us, length us, event | category | flops | bytes accessed | tf_op | source)
XLA Modules:
  0.0 50.0 jit_solution(13559437219355358913)
XLA Ops:
  0.6 44.1 %shard_map.84 = (bf16[256,2048]{1,0:T(8,128)(2,1)}, bf16[256,2048]{1,0:T(8,128)(2,1)}, bf16[256,512]{1,0:T(8,128)(2,1)}, bf16[256,512]{1,0:T(8,128)(2,1)}) custom-call(s32[64]{0:T(128)} %docs.1, bf16[256,2048]{1,0:T(8,128)(2,1)} %q_hbm.1, bf16[256,512]{1,0:T(8,128)(2,1)} %k_hbm.1, bf16[256,512]{1,0:T(8,128)(2,1)} %v_hbm.1, bf16[256,2048]{1,0:T(8,128)(2,1)} %g_hbm.1), custom_call_target="tpu_custom_call" | custom-call | flops 3300000000 | bytes 5500000 | tf_op jit(solution)/shard_map/pallas_call | solution.py:278
  44.8 0.0 copy-start
  44.8 2.4 %copy.13 = bf16[256,2048]{1,0:T(8,128)(2,1)} copy(bf16[256,2048]{1,0:T(8,128)(2,1)} %get-tuple-element.8) | data formatting | bytes 2097152
  47.2 0.0 copy-done
  47.2 0.0 copy-start.2
  47.2 1.0 %copy.14 = bf16[256,2048]{1,0:T(8,128)(2,1)} copy(bf16[256,2048]{1,0:T(8,128)(2,1)S(1)} %copy-done) | data formatting | bytes 2097152
  48.1 0.1 copy-done.2
  48.3 0.0 copy-start.1
  48.3 0.7 %copy.15 = bf16[256,512]{1,0:T(8,128)(2,1)} copy(bf16[256,512]{1,0:T(8,128)(2,1)S(1)} %copy-done.2) | data formatting | bytes 524288
  49.0 0.3 copy-done.1
  49.3 0.7 %copy.16 = bf16[256,512]{1,0:T(8,128)(2,1)} copy(bf16[256,512]{1,0:T(8,128)(2,1)S(1)} %copy-done.1) | data formatting | bytes 524288
Async XLA Ops:
  44.8 2.4 %copy-start = (bf16[256,2048]{1,0:T(8,128)(2,1)S(1)}, bf16[256,2048]{1,0:T(8,128)(2,1)}, u32[]{:S(2)}) copy-start(bf16[256,2048]{1,0:T(8,128)(2,1)} %get-tuple-element.9) | copy-start | bytes 3145732
  47.2 1.1 %copy-start.2 = (bf16[256,512]{1,0:T(8,128)(2,1)S(1)}, bf16[256,512]{1,0:T(8,128)(2,1)}, u32[]{:S(2)}) copy-start(bf16[256,512]{1,0:T(8,128)(2,1)} %get-tuple-element.10) | copy-start | bytes 786436
  48.3 1.0 %copy-start.1 = (bf16[256,512]{1,0:T(8,128)(2,1)S(1)}, bf16[256,512]{1,0:T(8,128)(2,1)}, u32[]{:S(2)}) copy-start(bf16[256,512]{1,0:T(8,128)(2,1)} %get-tuple-element.11) | copy-start | bytes 786436
where the time goes:
time: 50.2 us; the launch traced here: 50 us
  Pallas kernels  44.1 us (88%)
  local copies, waits for them, and re-layouts  5.23 us (10%)
  between operations  0.65 us (1%)
    pallas_call x1, Pallas kernels, on_device(): pl.pallas_call(kernel, out_shape=[jax.ShapeDtypeStruct(queries.shape, bf1...  44.1 us
    unnamed x10, local copies, waits for them, and re-layouts  5.23 us

commit v1 on v0

v1 whole, which is shorter than its diff:
```python
import math

import jax
import jax.numpy as jnp
from jax import lax
from jax.experimental import pallas as pl
from jax.experimental.pallas import tpu as pltpu
from jax.sharding import PartitionSpec as P

HEAD_DIM = 128
HEADS = 16
KV_HEADS = 4
GROUP = HEADS // KV_HEADS
BLOCK = 128
MOST = 4
PIECES = 4
PIECE = 64
ROWS = 256
LEAD = (MOST - 1) * BLOCK
WINDOW = MOST * BLOCK
SCALE = 1.0 / math.sqrt(HEAD_DIM)
SCALE_LOG2 = math.log2(math.e) / math.sqrt(HEAD_DIM)
FAR = 1e30
MESH = pl.DeviceIdType.MESH

NT = (((1,), (1,)), ((), ()))
TN = (((0,), (0,)), ((), ()))
NN = (((1,), (0,)), ((), ()))


def dot(lhs, rhs, dims):
    return lax.dot_general(lhs, rhs, dims, preferred_element_type=jnp.float32)


def block_rows(value, index):
    return value[index * BLOCK : (index + 1) * BLOCK]


def attend(keys, values, queries, grads, live):
    width = queries.shape[0]
    scores = dot(keys, queries, NT)
    weight_grad = dot(values, grads, NT)
    causal = lax.broadcasted_iota(jnp.int32, (BLOCK, BLOCK), 0) <= lax.broadcasted_iota(
        jnp.int32, (BLOCK, BLOCK), 1
    )
    exps, inverses = [], []
    for lane in range(0, width, BLOCK):
        tiles = [block_rows(scores, t)[:, lane : lane + BLOCK] for t in range(MOST)]
        tiles[-1] = jnp.where(causal, tiles[-1], -FAR)
        top = jnp.max(tiles[-1], axis=0, keepdims=True)
        for t in range(MOST - 1):
            top = jnp.maximum(top, jnp.where(live[t], jnp.max(tiles[t], axis=0, keepdims=True), -FAR))
        top = top * SCALE_LOG2
        shifts = [jnp.where(live[t], top, FAR) for t in range(MOST - 1)] + [top]
        parts = [jnp.exp2(tiles[t] * SCALE_LOG2 - shifts[t]) for t in range(MOST)]
        inverses.append(1.0 / jnp.sum(sum(parts), axis=0, keepdims=True))
        exps.append(jnp.concatenate([p.astype(jnp.bfloat16) for p in parts], 0))
    exps = jnp.concatenate(exps, 1)
    inverse = jnp.concatenate(inverses, 1)
    attended = dot(values, exps, TN) * inverse
    row_dot = jnp.sum(attended * jnp.transpose(grads).astype(jnp.float32), axis=0, keepdims=True)
    score_grad = []
    for lane in range(0, width, BLOCK):
        lanes = slice(lane, lane + BLOCK)
        score_grad.append(
            jnp.concatenate(
                [
                    block_rows(exps, t)[:, lanes]
                    * (block_rows(weight_grad, t)[:, lanes] - row_dot[:, lanes]).astype(jnp.bfloat16)
                    for t in range(MOST)
                ],
                0,
            )
        )
    score_grad = jnp.concatenate(score_grad, 1)
    column = jnp.transpose(jnp.broadcast_to(inverse, (BLOCK, width)))
    value_part = dot(exps, (grads.astype(jnp.float32) * column).astype(jnp.bfloat16), NN)
    key_part = dot(score_grad, (queries.astype(jnp.float32) * column).astype(jnp.bfloat16), NN)

    def outputs():
        query_grad = dot(keys, score_grad, TN) * (inverse * SCALE)
        return (
            jnp.transpose(attended.astype(jnp.bfloat16)),
            jnp.transpose(query_grad.astype(jnp.bfloat16)),
        )

    return key_part * SCALE, value_part, outputs


def kernel(
    docs_hbm, q_hbm, k_hbm, v_hbm, g_hbm, att_buf, dq_buf, dk_buf, dv_buf,
    docs, q_buf, g_buf, kv_buf, part, own_part, send_buf, got_buf,
    load_sem, kv_sem,
    first_send, first_recv, own_send, own_recv, fwd_send, fwd_recv, ret_send, ret_recv,
):
    seq = lax.axis_index("seq")
    me = lax.axis_index("ctx")
    last = lax.axis_size("ctx") - 1
    has_prev, has_next = me > 0, me < last
    prev, following = jnp.maximum(me - 1, 0), jnp.minimum(me + 1, last)

    barrier = pltpu.get_barrier_semaphore()

    @pl.when(has_prev)
    def _():
        pl.semaphore_signal(barrier, inc=1, device_id=(seq, prev), device_id_type=MESH)

    kv_loads = []
    for h in range(KV_HEADS):
        for n, ref in enumerate((k_hbm, v_hbm)):
            copy = pltpu.make_async_copy(
                ref.at[:, pl.ds(h * HEAD_DIM, HEAD_DIM)],
                kv_buf.at[h, n, pl.ds(LEAD, ROWS)],
                kv_sem.at[h, n],
            )
            copy.start()
            kv_loads.append(copy)
    loads = [
        pltpu.make_async_copy(q_hbm, q_buf, load_sem.at[0]),
        pltpu.make_async_copy(g_hbm, g_buf, load_sem.at[1]),
        pltpu.make_async_copy(docs_hbm, docs, load_sem.at[2]),
    ]
    for copy in loads:
        copy.start()

    def own(h, b):
        return pltpu.make_async_remote_copy(
            kv_buf.at[h, :, pl.ds(LEAD + b * BLOCK, BLOCK)],
            kv_buf.at[h, :, pl.ds((1 + b) * BLOCK, BLOCK)],
            own_send.at[h, b], own_recv.at[h, b],
            device_id=(seq, following), device_id_type=MESH,
        )

    def first(p):
        n, rows = p // 2, p % 2 * PIECE
        return pltpu.make_async_remote_copy(
            (k_hbm, v_hbm)[n].at[pl.ds(BLOCK + rows, PIECE), pl.ds(0, HEAD_DIM)],
            kv_buf.at[0, n, pl.ds(2 * BLOCK + rows, PIECE)],
            first_send.at[p], first_recv.at[p],
            device_id=(seq, following), device_id_type=MESH,
        )

    def forward(h):
        return pltpu.make_async_remote_copy(
            kv_buf.at[h, :, pl.ds(2 * BLOCK, BLOCK)],
            kv_buf.at[h, :, pl.ds(0, BLOCK)],
            fwd_send.at[h], fwd_recv.at[h],
            device_id=(seq, following), device_id_type=MESH,
        )

    def forward_first(p):
        n, rows = p // 2, p % 2 * PIECE
        return pltpu.make_async_remote_copy(
            kv_buf.at[0, n, pl.ds(2 * BLOCK + rows, PIECE)],
            kv_buf.at[0, n, pl.ds(rows, PIECE)],
            first_send.at[PIECES + p], first_recv.at[PIECES + p],
            device_id=(seq, following), device_id_type=MESH,
        )

    def give_back(h, b, n):
        return pltpu.make_async_remote_copy(
            send_buf.at[h, b, n], got_buf.at[h, b, n],
            ret_send.at[h, b, n], ret_recv.at[h, b, n],
            device_id=(seq, prev), device_id_type=MESH,
        )

    def next_first(h):
        @pl.when(has_next)
        def _():
            own(h, 1).start()

    def next_second(h):
        @pl.when(has_next)
        def _():
            own(h, 0).start()

    @pl.when(has_next)
    def _():
        pl.semaphore_wait(barrier, 1)
        for p in range(PIECES):
            first(p).start()

    for copy in kv_loads:
        copy.wait()

    next_second(0)

    @pl.when(jnp.logical_not(has_prev))
    def _():
        kv_buf[:, :, :LEAD] = jnp.zeros((KV_HEADS, 2, LEAD, HEAD_DIM), jnp.bfloat16)

    for copy in loads:
        copy.wait()

    def live(slot):
        own_doc = docs[2 * me + slot]
        result = []
        for t in range(MOST - 1):
            place = 2 * me + slot + t - (MOST - 1)
            result.append((place >= 0) & (docs[jnp.maximum(place, 0)] == own_doc))
        return result

    lives = [live(0), live(1)]

    def compute(h, slot):
        rows = slice(slot * BLOCK, (slot + 1) * BLOCK)
        lanes = [slice((h * GROUP + j) * HEAD_DIM, (h * GROUP + j + 1) * HEAD_DIM) for j in range(GROUP)]
        queries = jnp.concatenate([q_buf[rows, lane] for lane in lanes], 0)
        grads = jnp.concatenate([g_buf[rows, lane] for lane in lanes], 0)
        keys = kv_buf[h, 0, slot * BLOCK : slot * BLOCK + WINDOW]
        values = kv_buf[h, 1, slot * BLOCK : slot * BLOCK + WINDOW]
        key_part, value_part, outputs = attend(keys, values, queries, grads, lives[slot])

        def write():
            attended, query_grad = outputs()
            for j, lane in enumerate(lanes):
                att_buf[rows, lane] = block_rows(attended, j)
                dq_buf[rows, lane] = block_rows(query_grad, j)

        return (key_part, value_part), write

    def relay(h):
        @pl.when(has_next)
        def _():
            for n in (1, 0):
                give_back(h, 0, n).wait_recv()
                send_buf[h, 2, n] = (part[h, n] + got_buf[h, 0, n].astype(jnp.float32)).astype(jnp.bfloat16)

                @pl.when(has_prev)
                def _(n=n):
                    give_back(h, 2, n).start()

        @pl.when(jnp.logical_not(has_next))
        def _():
            send_buf[h, 2] = part[h].astype(jnp.bfloat16)
            for n in (1, 0):
                give_back(h, 2, n).start()

    def finish(h):
        @pl.when(has_next)
        def _():
            for b in range(2):
                for n in range(2):
                    give_back(h, 1 + b, n).wait_recv()
                own_part[h, b] += got_buf[h, 1 + b].astype(jnp.float32)

        for n, ref in enumerate((dk_buf, dv_buf)):
            for b in range(2):
                ref[b * BLOCK : (b + 1) * BLOCK, h * HEAD_DIM : (h + 1) * HEAD_DIM] = own_part[
                    h, b, n
                ].astype(jnp.bfloat16)

    def pass_on(h):
        if h == 0:
            for p in range(PIECES):

                @pl.when(has_prev)
                def _(p=p):
                    first(p).wait_recv()

                @pl.when(has_next)
                def _(p=p):
                    forward_first(p).start()
        else:

            @pl.when(has_prev)
            def _():
                own(h, 1).wait_recv()

            @pl.when(has_next)
            def _():
                forward(h).start()

    def slot_one(h):
        @pl.when(has_prev)
        def _():
            own(h, 0).wait_recv()

        sums, write = compute(h, 1)
        for n in range(2):
            part[h, n] = block_rows(sums[n], 1)
            own_part[h, 0, n] = block_rows(sums[n], 2)
            own_part[h, 1, n] = block_rows(sums[n], 3)
            own_part[h, 2, n] = block_rows(sums[n], 0)
        write()

    def slot_zero(h):
        @pl.when(has_prev)
        def _():
            if h == 0:
                for p in range(PIECES):
                    forward_first(p).wait_recv()
            else:
                forward(h).wait_recv()

        sums, write = compute(h, 0)
        for n in range(2):
            send_buf[h, 0, n] = block_rows(sums[n], 0).astype(jnp.bfloat16)
            send_buf[h, 1, n] = (block_rows(sums[n], 1) + own_part[h, 2, n]).astype(jnp.bfloat16)

        @pl.when(has_prev)
        def _():
            for b in range(2):
                for n in (1, 0):
                    give_back(h, b, n).start()

        for n in range(2):
            part[h, n] += block_rows(sums[n], 2)
            own_part[h, 0, n] += block_rows(sums[n], 3)
        write()

    order = (
        (next_first, 1),
        (pass_on, 0),
        (next_first, 2),
        (next_second, 1),
        (pass_on, 1),
        (next_second, 2),
        (next_first, 3),
        (slot_one, 0),
        (slot_zero, 0),
        (pass_on, 2),
        (slot_one, 1),
        (slot_zero, 1),
        (next_second, 3),
        (slot_one, 2),
        (pass_on, 3),
        (relay, 0),
        (slot_zero, 2),
        (slot_one, 3),
        (slot_zero, 3),
        (relay, 1),
        (relay, 2),
        (relay, 3),
        (finish, 2),
        (finish, 1),
        (finish, 0),
        (finish, 3),
    )
    for step, h in order:
        step(h)

    @pl.when(has_next)
    def _():
        for p in range(PIECES):
            first(p).wait_send()
            forward_first(p).wait_send()
        for h in range(KV_HEADS):
            own(h, 0).wait_send()
            if h > 0:
                own(h, 1).wait_send()
                forward(h).wait_send()

    @pl.when(has_prev)
    def _():
        for h in range(KV_HEADS):
            for b in range(3):
                for n in range(2):
                    give_back(h, b, n).wait_send()

def write_out(*refs):
    count = len(refs) // 2
    sem = refs[-1]
    copies = [pltpu.make_async_copy(refs[n], refs[count + n], sem.at[n]) for n in range(count)]
    for copy in copies:
        copy.start()
    for copy in copies:
        copy.wait()


def on_device(queries, keys, values, out_grad, block_docs):
    hbm = pl.BlockSpec(memory_space=pl.ANY)
    dma = pltpu.SemaphoreType.DMA
    bf16, f32 = jnp.bfloat16, jnp.float32
    vmem = pl.BlockSpec(memory_space=pltpu.VMEM)
    results = pl.pallas_call(
        kernel,
        out_shape=[
            pltpu.VMEM(queries.shape, bf16),
            pltpu.VMEM(queries.shape, bf16),
            pltpu.VMEM(keys.shape, bf16),
            pltpu.VMEM(keys.shape, bf16),
        ],
        in_specs=[hbm] * 5,
        out_specs=[vmem] * 4,
        scratch_shapes=[
            pltpu.SMEM(block_docs.shape, jnp.int32),
            pltpu.VMEM((ROWS, HEADS * HEAD_DIM), bf16),
            pltpu.VMEM((ROWS, HEADS * HEAD_DIM), bf16),
            pltpu.VMEM((KV_HEADS, 2, LEAD + ROWS, HEAD_DIM), bf16),
            pltpu.VMEM((KV_HEADS, 2, BLOCK, HEAD_DIM), f32),
            pltpu.VMEM((KV_HEADS, 3, 2, BLOCK, HEAD_DIM), f32),
            pltpu.VMEM((KV_HEADS, 3, 2, BLOCK, HEAD_DIM), bf16),
            pltpu.VMEM((KV_HEADS, 3, 2, BLOCK, HEAD_DIM), bf16),
            dma((3,)),
            dma((KV_HEADS, 2)),
            dma((2 * PIECES,)),
            dma((2 * PIECES,)),
            dma((KV_HEADS, 2)),
            dma((KV_HEADS, 2)),
            dma((KV_HEADS,)),
            dma((KV_HEADS,)),
            dma((KV_HEADS, 3, 2)),
            dma((KV_HEADS, 3, 2)),
        ],
        compiler_params=pltpu.CompilerParams(
            collective_id=0, has_side_effects=True, vmem_limit_bytes=40 * 1024 * 1024
        ),
        cost_estimate=pl.CostEstimate(
            flops=3_300_000_000, bytes_accessed=5_500_000, transcendentals=2_100_000
        ),
    )(*(pltpu.with_memory_space_constraint(x, pltpu.HBM) for x in (block_docs, queries, keys, values, out_grad)))
    return pl.pallas_call(
        write_out,
        out_shape=[pltpu.HBM(value.shape, value.dtype) for value in results],
        in_specs=[vmem] * 4,
        out_specs=[hbm] * 4,
        scratch_shapes=[dma((4,))],
    )(*(pltpu.with_memory_space_constraint(x, pltpu.VMEM) for x in results))


def solution(mesh):
    tokens = P(("seq", "ctx"), None)
    return jax.shard_map(
        on_device,
        mesh=mesh,
        in_specs=(tokens, tokens, tokens, tokens, P("seq")),
        out_specs=(tokens, tokens, tokens, tokens),
        check_vma=False,
    )
```

time: 50.2 us -> 36.5 us (0.73)
  the two profiles are of different devices: /device:TPU:12 before, /device:TPU:66 now
where the time goes in v1:
time: 36.5 us; the launch traced here: 36.1 us
  Pallas kernels  35.4 us (97%)
  between operations  0.64 us (2%)
    pallas_call x1, Pallas kernels, on_device(): pl.pallas_call(kernel, out_shape=[pltpu.VMEM(queries.shape, bf16), pltpu....  33.9 us
    pallas_call x1, Pallas kernels, on_device(): pl.pallas_call(write_out, out_shape=[pltpu.HBM(value.shape, value.dtype)...  1.52 us

profile of v1, /device:TPU:66, one launch (start us, length us, event | category | flops | bytes accessed | tf_op | source)
XLA Modules:
  0.0 36.1 jit_solution(15425723563494077971)
XLA Ops:
  0.6 33.9 %shard_map.84 = (bf16[256,2048]{1,0:T(8,128)(2,1)S(1)}, bf16[256,2048]{1,0:T(8,128)(2,1)S(1)}, bf16[256,512]{1,0:T(8,128)(2,1)S(1)}, bf16[256,512]{1,0:T(8,128)(2,1)S(1)}) custom-call(s32[64]{0:T(128)} %docs_hbm.1, bf16[256,2048]{1,0:T(8,128)(2,1)} %q_hbm.1, bf16[256,512]{1,0:T(8,128)(2,1)} %k_hbm.1, bf16[256,512]{1,0:T(8,128)(2,1)} %v_hbm.1, ...), custom_call_target="tpu_custom_call" | custom-call | flops 3300000000 | bytes 5500000 | tf_op jit(solution)/shard_map/pallas_call | solution.py:376
  34.6 1.5 %shard_map.85 = (bf16[256,2048]{1,0:T(8,128)(2,1)}, bf16[256,2048]{1,0:T(8,128)(2,1)}, bf16[256,512]{1,0:T(8,128)(2,1)}, bf16[256,512]{1,0:T(8,128)(2,1)}) custom-call(bf16[256,2048]{1,0:T(8,128)(2,1)S(1)} %get-tuple-element.8.refs_0_, bf16[256,2048]{1,0:T(8,128)(2,1)S(1)} %get-tuple-element.9.refs_1_, bf16[256,512]{1,0:T(8,128)(2,1)S(1)} %get-tuple-element.10.refs_2_, ...), custom_call_target="tpu_custom_call" | custom-call | tf_op jit(solution)/shard_map/pallas_call | solution.py:413

commit v2 on v1

--- a/solution.py
+++ b/solution.py
@@ -164,6 +164,13 @@
             device_id=(seq, prev), device_id_type=MESH,
         )
 
+    def give_back_b(h):
+        return pltpu.make_async_remote_copy(
+            send_buf.at[h, 1], got_buf.at[h, 1],
+            ret_send.at[h, 1, 0], ret_recv.at[h, 1, 0],
+            device_id=(seq, prev), device_id_type=MESH,
+        )
+
     def next_first(h):
         @pl.when(has_next)
         def _():
@@ -183,7 +190,6 @@
     for copy in kv_loads:
         copy.wait()
 
-    next_second(0)
 
     @pl.when(jnp.logical_not(has_prev))
     def _():
@@ -239,9 +245,10 @@
     def finish(h):
         @pl.when(has_next)
         def _():
+            give_back_b(h).wait_recv()
+            for n in range(2):
+                give_back(h, 2, n).wait_recv()
             for b in range(2):
-                for n in range(2):
-                    give_back(h, 1 + b, n).wait_recv()
                 own_part[h, b] += got_buf[h, 1 + b].astype(jnp.float32)
 
         for n, ref in enumerate((dk_buf, dv_buf)):
@@ -270,6 +277,14 @@
             @pl.when(has_next)
             def _():
                 forward(h).start()
+
+    unwritten = {}
+
+    def write_one(h):
+        unwritten.pop((h, 1))()
+
+    def write_zero(h):
+        unwritten.pop((h, 0))()
 
     def slot_one(h):
         @pl.when(has_prev)
@@ -282,7 +297,7 @@
             own_part[h, 0, n] = block_rows(sums[n], 2)
             own_part[h, 1, n] = block_rows(sums[n], 3)
             own_part[h, 2, n] = block_rows(sums[n], 0)
-        write()
+        unwritten[h, 1] = write
 
     def slot_zero(h):
         @pl.when(has_prev)
@@ -300,63 +315,83 @@
 
         @pl.when(has_prev)
         def _():
-            for b in range(2):
-                for n in (1, 0):
-                    give_back(h, b, n).start()
+            for n in (1, 0):
+                give_back(h, 0, n).start()
+            give_back_b(h).start()
 
         for n in range(2):
             part[h, n] += block_rows(sums[n], 2)
             own_part[h, 0, n] += block_rows(sums[n], 3)
-        write()
+        unwritten[h, 0] = write
+
+    def drain(h):
+        @pl.when(has_next)
+        def _():
+            for p in range(PIECES):
+                first(p).wait_send()
+                forward_first(p).wait_send()
+            for g in range(KV_HEADS):
+                own(g, 0).wait_send()
+                if g > 0:
+                    own(g, 1).wait_send()
+                    forward(g).wait_send()
+
+        @pl.when(has_prev)
+        def _():
+            for g in range(KV_HEADS):
+                give_back_b(g).wait_send()
+                for b in (0,) if g == h else (0, 2):
+                    for n in range(2):
+                        give_back(g, b, n).wait_send()
 
     order = (
         (next_first, 1),
+        (next_second, 0),
         (pass_on, 0),
-        (next_first, 2),
         (next_second, 1),
         (pass_on, 1),
+        (slot_one, 0),
+        (write_one, 0),
+        (next_first, 2),
+        (slot_zero, 0),
+        (next_first, 3),
         (next_second, 2),
-        (next_first, 3),
-        (slot_one, 0),
-        (slot_zero, 0),
-        (pass_on, 2),
         (slot_one, 1),
         (slot_zero, 1),
+        (pass_on, 2),
+        (write_one, 1),
         (next_second, 3),
+        (relay, 0),
+        (pass_on, 3),
         (slot_one, 2),
-        (pass_on, 3),
-        (relay, 0),
+        (relay, 1),
         (slot_zero, 2),
+        (write_one, 2),
         (slot_one, 3),
         (slot_zero, 3),
-        (relay, 1),
+        (write_zero, 0),
+        (write_one, 3),
+        (finish, 1),
+        (write_zero, 3),
+        (write_zero, 1),
+        (finish, 0),
         (relay, 2),
         (relay, 3),
+        (drain, 3),
         (finish, 2),
-        (finish, 1),
-        (finish, 0),
+        (write_zero, 2),
         (finish, 3),
     )
     for step, h in order:
         step(h)
 
-    @pl.when(has_next)
-    def _():
-        for p in range(PIECES):
-            first(p).wait_send()
-            forward_first(p).wait_send()
-        for h in range(KV_HEADS):
-            own(h, 0).wait_send()
-            if h > 0:
-                own(h, 1).wait_send()
-                forward(h).wait_send()
+    final = KV_HEADS - 1
 
     @pl.when(has_prev)
     def _():
-        for h in range(KV_HEADS):
-            for b in range(3):
-                for n in range(2):
-                    give_back(h, b, n).wait_send()
+        for n in range(2):
+            give_back(final, 2, n).wait_send()
+
 
 def write_out(*refs):
     count = len(refs) // 2

time: 36.5 us -> 36.1 us (0.989)
  no operation moved by 1% of the time
where the time goes in v2:
time: 36.1 us; the launch traced here: 36 us
  Pallas kernels  35.4 us (98%)
  between operations  0.64 us (2%)
    pallas_call x1, Pallas kernels, on_device(): pl.pallas_call(kernel, out_shape=[pltpu.VMEM(queries.shape, bf16), pltpu....  33.9 us
    pallas_call x1, Pallas kernels, on_device(): pl.pallas_call(write_out, out_shape=[pltpu.HBM(value.shape, value.dtype)...  1.52 us

profile of v2, /device:TPU:66, one launch (start us, length us, event | category | flops | bytes accessed | tf_op | source)
XLA Modules:
  0.0 36.0 jit_solution(8937192361674119058)
XLA Ops:
  0.6 33.9 %shard_map.84 = (bf16[256,2048]{1,0:T(8,128)(2,1)S(1)}, bf16[256,2048]{1,0:T(8,128)(2,1)S(1)}, bf16[256,512]{1,0:T(8,128)(2,1)S(1)}, bf16[256,512]{1,0:T(8,128)(2,1)S(1)}) custom-call(s32[64]{0:T(128)} %docs_hbm.1, bf16[256,2048]{1,0:T(8,128)(2,1)} %q_hbm.1, bf16[256,512]{1,0:T(8,128)(2,1)} %k_hbm.1, bf16[256,512]{1,0:T(8,128)(2,1)} %v_hbm.1, ...), custom_call_target="tpu_custom_call" | custom-call | flops 3300000000 | bytes 5500000 | tf_op jit(solution)/shard_map/pallas_call | solution.py:411
  34.5 1.5 %shard_map.85 = (bf16[256,2048]{1,0:T(8,128)(2,1)}, bf16[256,2048]{1,0:T(8,128)(2,1)}, bf16[256,512]{1,0:T(8,128)(2,1)}, bf16[256,512]{1,0:T(8,128)(2,1)}) custom-call(bf16[256,2048]{1,0:T(8,128)(2,1)S(1)} %get-tuple-element.8.refs_0_, bf16[256,2048]{1,0:T(8,128)(2,1)S(1)} %get-tuple-element.9.refs_1_, bf16[256,512]{1,0:T(8,128)(2,1)S(1)} %get-tuple-element.10.refs_2_, ...), custom_call_target="tpu_custom_call" | custom-call | tf_op jit(solution)/shard_map/pallas_call | solution.py:448

commit v3 on v1

--- a/solution.py
+++ b/solution.py
@@ -183,7 +183,6 @@
     for copy in kv_loads:
         copy.wait()
 
-    next_second(0)
 
     @pl.when(jnp.logical_not(has_prev))
     def _():
@@ -271,6 +270,14 @@
             def _():
                 forward(h).start()
 
+    unwritten = {}
+
+    def write_one(h):
+        unwritten.pop((h, 1))()
+
+    def write_zero(h):
+        unwritten.pop((h, 0))()
+
     def slot_one(h):
         @pl.when(has_prev)
         def _():
@@ -282,7 +289,7 @@
             own_part[h, 0, n] = block_rows(sums[n], 2)
             own_part[h, 1, n] = block_rows(sums[n], 3)
             own_part[h, 2, n] = block_rows(sums[n], 0)
-        write()
+        unwritten[h, 1] = write
 
     def slot_zero(h):
         @pl.when(has_prev)
@@ -307,34 +314,43 @@
         for n in range(2):
             part[h, n] += block_rows(sums[n], 2)
             own_part[h, 0, n] += block_rows(sums[n], 3)
-        write()
+        unwritten[h, 0] = write
 
     order = (
         (next_first, 1),
+        (next_second, 0),
         (pass_on, 0),
-        (next_first, 2),
         (next_second, 1),
         (pass_on, 1),
+        (slot_one, 0),
+        (write_one, 0),
+        (next_first, 2),
+        (slot_zero, 0),
+        (next_first, 3),
         (next_second, 2),
-        (next_first, 3),
-        (slot_one, 0),
-        (slot_zero, 0),
-        (pass_on, 2),
         (slot_one, 1),
         (slot_zero, 1),
+        (pass_on, 2),
+        (write_one, 1),
         (next_second, 3),
+        (relay, 0),
+        (pass_on, 3),
         (slot_one, 2),
-        (pass_on, 3),
-        (relay, 0),
+        (relay, 1),
         (slot_zero, 2),
         (slot_one, 3),
         (slot_zero, 3),
-        (relay, 1),
         (relay, 2),
+        (write_one, 2),
+        (write_one, 3),
+        (write_zero, 0),
+        (finish, 1),
+        (write_zero, 3),
+        (write_zero, 1),
+        (finish, 0),
         (relay, 3),
         (finish, 2),
-        (finish, 1),
-        (finish, 0),
+        (write_zero, 2),
         (finish, 3),
     )
     for step, h in order:

time: 36.5 us -> 36.2 us (level)
  no operation moved by 1% of the time
where the time goes in v3:
time: 36.2 us; the launch traced here: 36.1 us
  Pallas kernels  35.4 us (98%)
  between operations  0.64 us (2%)
    pallas_call x1, Pallas kernels, on_device(): pl.pallas_call(kernel, out_shape=[pltpu.VMEM(queries.shape, bf16), pltpu....  33.9 us
    pallas_call x1, Pallas kernels, on_device(): pl.pallas_call(write_out, out_shape=[pltpu.HBM(value.shape, value.dtype)...  1.52 us

profile of v3, /device:TPU:66, one launch (start us, length us, event | category | flops | bytes accessed | tf_op | source)
XLA Modules:
  0.0 36.1 jit_solution(11974534206248738043)
XLA Ops:
  0.6 33.9 %shard_map.84 = (bf16[256,2048]{1,0:T(8,128)(2,1)S(1)}, bf16[256,2048]{1,0:T(8,128)(2,1)S(1)}, bf16[256,512]{1,0:T(8,128)(2,1)S(1)}, bf16[256,512]{1,0:T(8,128)(2,1)S(1)}) custom-call(s32[64]{0:T(128)} %docs_hbm.1, bf16[256,2048]{1,0:T(8,128)(2,1)} %q_hbm.1, bf16[256,512]{1,0:T(8,128)(2,1)} %k_hbm.1, bf16[256,512]{1,0:T(8,128)(2,1)} %v_hbm.1, ...), custom_call_target="tpu_custom_call" | custom-call | flops 3300000000 | bytes 5500000 | tf_op jit(solution)/shard_map/pallas_call | solution.py:392
  34.6 1.5 %shard_map.85 = (bf16[256,2048]{1,0:T(8,128)(2,1)}, bf16[256,2048]{1,0:T(8,128)(2,1)}, bf16[256,512]{1,0:T(8,128)(2,1)}, bf16[256,512]{1,0:T(8,128)(2,1)}) custom-call(bf16[256,2048]{1,0:T(8,128)(2,1)S(1)} %get-tuple-element.8.refs_0_, bf16[256,2048]{1,0:T(8,128)(2,1)S(1)} %get-tuple-element.9.refs_1_, bf16[256,512]{1,0:T(8,128)(2,1)S(1)} %get-tuple-element.10.refs_2_, ...), custom_call_target="tpu_custom_call" | custom-call | tf_op jit(solution)/shard_map/pallas_call | solution.py:429
